TPU v7x, 256 devices: a whole 4x4x8 slice. The times are simulated.
256 devices in a mesh: gx: 16 (over y, x_lo, core), gy: 16 (over z, x_hi).
Axes of the slice: x: 4 (x_hi: 2, x_lo: 2; x = x_hi * 2 + x_lo), y: 4, z: 8, core: 2. Of those that a mesh axis runs over, the one named last changes fastest.
Arguments:
- features: bfloat16 [128, 128, 2, 8, 256], P('gx', 'gy'), may hold values from -6 to 6
- cotangent: bfloat16 [128, 128, 2, 8, 256], P('gx', 'gy'), may hold values from -6 to 6
- weights: bfloat16 [27, 256, 256], replicated, may hold values from -0.078125 to 0.078125
- levels: int32 [16, 16, 2], P('gx', 'gy'), may hold values from 0 to 2, as said below
- counts: int32 [16, 16], P('gx', 'gy'), may hold values from 1 to 2, as said below
Outputs:
- output: bfloat16 [128, 128, 2, 8, 256], P('gx', 'gy')
- input_grad: bfloat16 [128, 128, 2, 8, 256], P('gx', 'gy')
- weight_grad: float32 [1769472], P(('gx', 'gy'))
Inputs may be any that keep to these rules, and one draw needn't show every extreme that they name: `levels`: slot s of a tile sits at level s or s + 1, the same shift for all slots of that tile. The active slots of a tile are its first counts slots.
All inputs are finite; a program needn't handle non-finite values.
Results may differ from a plain program's by a relative error of at most 0.001.
Values may be sent and summed in bfloat16 or wider, within the bound.
A program may use at most 128 MiB of HBM per device.

v0:
```python
import math

import jax
import jax.numpy as jnp
import numpy as np
from jax import lax
from jax.sharding import PartitionSpec as P


def with_halo(shard, sides, width):
    for axis, dim in sides:
        size, length = (lax.axis_size(axis), shard.shape[dim])
        up = [(i, (i + 1) % size) for i in range(size - 1)]
        down = [(j, i) for i, j in up]
        last = lax.slice_in_dim(shard, length - width, length, axis=dim)
        leading = lax.slice_in_dim(shard, 0, width, axis=dim)
        before = lax.ppermute(last, axis, up)
        after = lax.ppermute(leading, axis, down)
        shard = jnp.concatenate([before, shard, after], axis=dim)
    return shard


def assemble(window, near_levels, own_levels):
    extent = window.shape[0]
    column_map = np.array([0] + [1] * (extent - 2) + [2], dtype=np.int32)
    spread = near_levels[column_map][:, column_map]
    targets = own_levels[:, None] + jnp.array([-1, 0, 1], dtype=jnp.int32)[None, :]
    selector = (spread[:, :, None, None, :] == targets[None, None, :, :, None]).astype(jnp.bfloat16)
    stacked = jnp.einsum(
        "ijskr,ijrzc->ijskzc", selector, window, preferred_element_type=jnp.float32
    )
    below_layer = stacked[:, :, :, 0, -1:, :]
    same_level = stacked[:, :, :, 1]
    above_layer = stacked[:, :, :, 2, :1, :]
    return jnp.concatenate([below_layer, same_level, above_layer], axis=3).astype(jnp.bfloat16)


def convolve(frame, kernel, flipped):
    blocks = frame.shape[0] - 2
    summed = None
    for offset in range(27):
        step_x, step_y, step_z = (offset // 9, offset // 3 % 3, offset % 3)
        if flipped:
            step_x, step_y, step_z = (2 - step_x, 2 - step_y, 2 - step_z)
        sliced = frame[
            step_x : step_x + blocks, step_y : step_y + blocks, :, step_z : step_z + blocks, :
        ]
        if flipped:
            product = jnp.einsum(
                "xyszc,dc->xyszd", sliced, kernel[offset], preferred_element_type=jnp.float32
            )
        else:
            product = jnp.einsum(
                "xyszc,cd->xyszd", sliced, kernel[offset], preferred_element_type=jnp.float32
            )
        summed = product if summed is None else summed + product
    return summed


def weight_terms(frame, grads):
    blocks = grads.shape[0]
    terms = []
    for offset in range(27):
        step_x, step_y, step_z = (offset // 9, offset // 3 % 3, offset % 3)
        sliced = frame[
            step_x : step_x + blocks, step_y : step_y + blocks, :, step_z : step_z + blocks, :
        ]
        terms.append(
            jnp.einsum("xyszc,xyszd->cd", sliced, grads, preferred_element_type=jnp.float32)
        )
    return jnp.stack(terms)


def per_device(features, cotangent, weights, levels, counts):
    blocks = features.shape[0]
    slots = features.shape[2]
    slot_ids = jnp.arange(slots, dtype=jnp.int32)
    active = slot_ids < counts[0, 0]
    own_levels = jnp.where(active, levels[0, 0], jnp.full_like(levels[0, 0], -1000))
    near_levels = with_halo(own_levels.reshape(1, 1, slots), (("gx", 0), ("gy", 1)), 1)
    keep_mask = active[None, None, :, None, None]
    masked_cot = jnp.where(keep_mask, cotangent, jnp.zeros_like(cotangent))
    window_x = with_halo(features, (("gx", 0), ("gy", 1)), 1)
    window_g = with_halo(masked_cot, (("gx", 0), ("gy", 1)), 1)
    frame_x = assemble(window_x, near_levels, own_levels)
    frame_g = assemble(window_g, near_levels, own_levels)
    output = jnp.where(keep_mask, convolve(frame_x, weights, False), 0.0).astype(jnp.bfloat16)
    input_grad = jnp.where(keep_mask, convolve(frame_g, weights, True), 0.0).astype(jnp.bfloat16)
    grad_term = weight_terms(frame_x, masked_cot).reshape(-1)
    summed = lax.psum_scatter(grad_term, ("gx", "gy"), scatter_dimension=0, tiled=True)
    voxel_total = blocks * blocks * blocks * slots * lax.axis_size("gx") * lax.axis_size("gy")
    grad_scale = 1.0 / math.sqrt(voxel_total)
    weight_grad = summed * grad_scale
    return (output, input_grad, weight_grad)


def solution(mesh):
    return jax.shard_map(
        per_device,
        mesh=mesh,
        in_specs=(
            P("gx", "gy", None, None, None),
            P("gx", "gy", None, None, None),
            P(),
            P("gx", "gy", None),
            P("gx", "gy"),
        ),
        out_specs=(
            P("gx", "gy", None, None, None),
            P("gx", "gy", None, None, None),
            P(("gx", "gy")),
        ),
        check_vma=False,
    )
```

profile of v0, /device:TPU:1, one launch (start us, length us, event | category | flops | bytes accessed | tf_op | source)
XLA Modules:
  0.0 456.1 jit_solution(5375683518963448477)
XLA Ops:
  8.6 4.5 collective-permute-start
  13.1 1.9 collective-permute-start.1
  16.0 3.6 collective-permute-start.4
  19.7 1.9 collective-permute-start.5
  22.8 3.6 collective-permute-start.8
  28.5 1.9 collective-permute-start.9
  30.6 4.3 collective-permute-start.2
  37.0 4.8 %collective-permute-done.3 = s32[3,1,2]{1,2,0:T(2,128)S(1)} collective-permute-done((s32[3,1,2]{1,2,0:T(2,128)S(1)}, s32[3,1,2]{1,2,0:T(2,128)S(1)}, u32[]{:S(2)}, u32[]{:S(2)}) %collective-permute-start.3) | collective-permute-done | bytes 56 | tf_op jit(solution)/shard_map/ppermute | solution.py:18
  43.4 1.5 constant_dynamic-update-slice_fusion.1
  45.1 5.8 %collective-permute-start.6 = (bf16[10,1,2,8,256]{4,2,3,1,0:T(2,128)(2,1)S(1)}, bf16[10,1,2,8,256]{4,2,3,1,0:T(2,128)(2,1)S(1)}, u32[]{:S(2)}, u32[]{:S(2)}) collective-permute-start(bf16[10,1,2,8,256]{4,2,3,1,0:T(2,128)(2,1)S(1)} %get-tuple-element.36), channel_id=1, source_target_pairs={{0,1},{1,2},{2,3},{3,4},{4,5},{5,6},{6,7},{7,8},{8,9},{9,10},{10,1... | collective-permute-start | bytes 245768 | tf_op jit(solution)/shard_map/ppermute | solution.py:17
  52.3 5.5 %collective-permute-start.10 = (bf16[10,1,2,8,256]{4,3,2,1,0:T(8,128)(2,1)S(1)}, bf16[10,1,2,8,256]{4,3,2,1,0:T(8,128)(2,1)S(1)}, u32[]{:S(2)}, u32[]{:S(2)}) collective-permute-start(bf16[10,1,2,8,256]{4,3,2,1,0:T(8,128)(2,1)S(1)} %get-tuple-element.34), channel_id=1, source_target_pairs={{0,1},{1,2},{2,3},{3,4},{4,5},{5,6},{6,7},{7,8},{8,9},{9,10},{10,1... | collective-permute-start | bytes 245768 | tf_op jit(solution)/shard_map/ppermute | solution.py:17
  59.1 2.3 convolution_convert_fusion.1
  61.8 2.0 slice.503
  64.6 2.8 convolution_convert_fusion
  67.5 2.0 slice.539
  70.1 1.4 fusion.101
  71.5 1.5 fusion.98
  73.0 1.4 fusion.104
  77.2 1.5 fusion.107
  80.0 1.4 fusion.110
  81.4 1.4 fusion.83
  82.9 1.4 fusion.113
  85.7 1.4 fusion.116
  89.8 1.4 fusion.95
  91.2 1.4 fusion.136
  93.6 2.3 fusion.127
  98.2 3.0 fusion.119
  150.5 9.7 %copy.335 = f32[864,2,8,128]{3,1,2,0:T(2,128)} copy(f32[864,2,8,128]{3,2,1,0:T(8,128)} %bitcast.286) | data formatting | bytes 14155776
  160.3 2.4 fusion.17
  163.5 1.7 fusion.15
  188.1 259.5 %all-reduce.3.cloned.1.call-done = f32[1769472]{0:T(1024)} async-done(((f32[1769472]{0:T(1024)}), f32[1769472]{0:T(1024)}) %all-reduce.3.cloned.1.call-update) | async-done | bytes 7077904
  447.6 1.4 dynamic-slice_multiply_fusion
  (185 shorter events, 97.7 us)
Async XLA Ops:
  7.2 440.5 %all-reduce.3.cloned.1.call-start = ((), (), s32[]{:S(2)}) async-start(), calls=%async_computation | async-start | bytes 14155776
  8.6 19.9 %collective-permute-start = (s32[1,1,2]{0,2,1:T(2,128)S(1)}, s32[1,1,2]{0,2,1:T(2,128)S(1)}, u32[]{:S(2)}, u32[]{:S(2)}) collective-permute-start(s32[1,1,2]{0,2,1:T(2,128)S(1)} %compare_select_fusion), channel_id=1, source_target_pairs={{0,16},{16,32},{32,48},{48,64},{64,80},{80,96},{96,112},{112,128},... | collective-permute-start | bytes 32 | tf_op jit(solution)/shard_map/ppermute | solution.py:17
  13.1 17.3 %collective-permute-start.1 = (s32[1,1,2]{0,2,1:T(2,128)S(1)}, s32[1,1,2]{0,2,1:T(2,128)S(1)}, u32[]{:S(2)}, u32[]{:S(2)}) collective-permute-start(s32[1,1,2]{0,2,1:T(2,128)S(1)} %compare_select_fusion), channel_id=1, source_target_pairs={{16,0},{32,16},{48,32},{64,48},{80,64},{96,80},{112,96},{128,112},... | collective-permute-start | bytes 32 | tf_op jit(solution)/shard_map/ppermute | solution.py:18
  16.0 27.3 %collective-permute-start.4 = (bf16[1,8,2,8,256]{4,2,3,1,0:T(2,128)(2,1)S(1)}, bf16[1,8,2,8,256]{4,2,3,1,0:T(2,128)(2,1)S(1)}, u32[]{:S(2)}, u32[]{:S(2)}) collective-permute-start(bf16[1,8,2,8,256]{4,2,3,1,0:T(2,128)(2,1)S(1)} %copy.449), channel_id=1, source_target_pairs={{0,16},{16,32},{32,48},{48,64},{64,80},{80,96},{96,112},{112,128},... | collective-permute-start | bytes 196616 | tf_op jit(solution)/shard_map/ppermute | solution.py:17
  19.7 25.2 %collective-permute-start.5 = (bf16[1,8,2,8,256]{4,2,3,1,0:T(2,128)(2,1)S(1)}, bf16[1,8,2,8,256]{4,2,3,1,0:T(2,128)(2,1)S(1)}, u32[]{:S(2)}, u32[]{:S(2)}) collective-permute-start(bf16[1,8,2,8,256]{4,2,3,1,0:T(2,128)(2,1)S(1)} %copy.450), channel_id=1, source_target_pairs={{16,0},{32,16},{48,32},{64,48},{80,64},{96,80},{112,96},{128,112},... | collective-permute-start | bytes 196616 | tf_op jit(solution)/shard_map/ppermute | solution.py:18
  21.6 15.4 %copy-start.34 = (pred[2]{0:T(512)(128)(4,1)}, pred[2]{0:T(512)(128)(4,1)S(1)}, u32[]{:S(2)}) copy-start(pred[2]{0:T(512)(128)(4,1)S(1)} %iota_compare_fusion) | copy-start | bytes 10
  22.8 29.4 %collective-permute-start.8 = (bf16[1,8,2,8,256]{4,3,2,1,0:T(8,128)(2,1)S(1)}, bf16[1,8,2,8,256]{4,3,2,1,0:T(8,128)(2,1)S(1)}, u32[]{:S(2)}, u32[]{:S(2)}) collective-permute-start(bf16[1,8,2,8,256]{4,3,2,1,0:T(8,128)(2,1)S(1)} %get-tuple-element.38), channel_id=1, source_target_pairs={{0,16},{16,32},{32,48},{48,64},{64,80},{80,96},{96,112},{112,128},... | collective-permute-start | bytes 196616 | tf_op jit(solution)/shard_map/ppermute | solution.py:17
  28.5 23.7 %collective-permute-start.9 = (bf16[1,8,2,8,256]{4,3,2,1,0:T(8,128)(2,1)S(1)}, bf16[1,8,2,8,256]{4,3,2,1,0:T(8,128)(2,1)S(1)}, u32[]{:S(2)}, u32[]{:S(2)}) collective-permute-start(bf16[1,8,2,8,256]{4,3,2,1,0:T(8,128)(2,1)S(1)} %get-tuple-element.39), channel_id=1, source_target_pairs={{16,0},{32,16},{48,32},{64,48},{80,64},{96,80},{112,96},{128,112},... | collective-permute-start | bytes 196616 | tf_op jit(solution)/shard_map/ppermute | solution.py:18
  30.6 5.1 %collective-permute-start.2 = (s32[3,1,2]{1,2,0:T(2,128)S(1)}, s32[3,1,2]{1,2,0:T(2,128)S(1)}, u32[]{:S(2)}, u32[]{:S(2)}) collective-permute-start(s32[3,1,2]{1,2,0:T(2,128)S(1)} %copy.207), channel_id=1, source_target_pairs={{0,1},{1,2},{2,3},{3,4},{4,5},{5,6},{6,7},{7,8},{8,9},{9,10},{10,1... | collective-permute-start | bytes 80 | tf_op jit(solution)/shard_map/ppermute | solution.py:17
  35.7 6.1 %collective-permute-start.3 = (s32[3,1,2]{1,2,0:T(2,128)S(1)}, s32[3,1,2]{1,2,0:T(2,128)S(1)}, u32[]{:S(2)}, u32[]{:S(2)}) collective-permute-start(s32[3,1,2]{1,2,0:T(2,128)S(1)} %copy.207), channel_id=1, source_target_pairs={{1,0},{2,1},{3,2},{4,3},{5,4},{6,5},{7,6},{8,7},{9,8},{10,9},{11,1... | collective-permute-start | bytes 80 | tf_op jit(solution)/shard_map/ppermute | solution.py:18
  45.1 14.0 %collective-permute-start.6 = (bf16[10,1,2,8,256]{4,2,3,1,0:T(2,128)(2,1)S(1)}, bf16[10,1,2,8,256]{4,2,3,1,0:T(2,128)(2,1)S(1)}, u32[]{:S(2)}, u32[]{:S(2)}) collective-permute-start(bf16[10,1,2,8,256]{4,2,3,1,0:T(2,128)(2,1)S(1)} %get-tuple-element.36), channel_id=1, source_target_pairs={{0,1},{1,2},{2,3},{3,4},{4,5},{5,6},{6,7},{7,8},{8,9},{9,10},{10,1... | collective-permute-start | bytes 245768 | tf_op jit(solution)/shard_map/ppermute | solution.py:17
  50.9 8.2 %collective-permute-start.7 = (bf16[10,1,2,8,256]{4,2,3,1,0:T(2,128)(2,1)S(1)}, bf16[10,1,2,8,256]{4,2,3,1,0:T(2,128)(2,1)S(1)}, u32[]{:S(2)}, u32[]{:S(2)}) collective-permute-start(bf16[10,1,2,8,256]{4,2,3,1,0:T(2,128)(2,1)S(1)} %get-tuple-element.37), channel_id=1, source_target_pairs={{1,0},{2,1},{3,2},{4,3},{5,4},{6,5},{7,6},{8,7},{9,8},{10,9},{11,1... | collective-permute-start | bytes 245768 | tf_op jit(solution)/shard_map/ppermute | solution.py:18
  52.3 11.5 %collective-permute-start.10 = (bf16[10,1,2,8,256]{4,3,2,1,0:T(8,128)(2,1)S(1)}, bf16[10,1,2,8,256]{4,3,2,1,0:T(8,128)(2,1)S(1)}, u32[]{:S(2)}, u32[]{:S(2)}) collective-permute-start(bf16[10,1,2,8,256]{4,3,2,1,0:T(8,128)(2,1)S(1)} %get-tuple-element.34), channel_id=1, source_target_pairs={{0,1},{1,2},{2,3},{3,4},{4,5},{5,6},{6,7},{7,8},{8,9},{9,10},{10,1... | collective-permute-start | bytes 245768 | tf_op jit(solution)/shard_map/ppermute | solution.py:17
  57.8 6.7 %collective-permute-start.11 = (bf16[10,1,2,8,256]{4,3,2,1,0:T(8,128)(2,1)S(1)}, bf16[10,1,2,8,256]{4,3,2,1,0:T(8,128)(2,1)S(1)}, u32[]{:S(2)}, u32[]{:S(2)}) collective-permute-start(bf16[10,1,2,8,256]{4,3,2,1,0:T(8,128)(2,1)S(1)} %get-tuple-element.35), channel_id=1, source_target_pairs={{1,0},{2,1},{3,2},{4,3},{5,4},{6,5},{7,6},{8,7},{9,8},{10,9},{11,1... | collective-permute-start | bytes 245768 | tf_op jit(solution)/shard_map/ppermute | solution.py:18
  67.4 2.6 copy-start.2
  69.8 22.8 %copy-start = (bf16[10,10,2,1,256]{4,3,2,1,0:T(2,128)(2,1)}, bf16[10,10,2,1,256]{4,3,2,1,0:T(2,128)(2,1)S(1)}, u32[]{:S(2)}) copy-start(bf16[10,10,2,1,256]{4,3,2,1,0:T(2,128)(2,1)S(1)} %get-tuple-element.4) | copy-start | bytes 307204
  160.2 3.0 copy-start.3
  160.3 3.3 copy-start.13
  163.5 1.7 copy-start.14
  163.5 1.9 copy-start.15
  165.4 1.5 copy-start.12
  166.9 1.5 copy-start.10
  168.5 1.5 copy-start.8
  170.0 1.5 copy-start.6
  173.7 1.5 copy-start.16
  173.7 1.5 copy-start.17
  173.7 2.0 copy-start.18
  174.1 2.1 copy-start.19
  174.1 2.4 copy-start.20
  176.5 1.5 copy-start.22
  179.6 1.5 copy-start.26
  184.2 1.6 copy-start.32
  (17 other events, 21.6 us)
Sparse Core Ops, SparseCore 0:
  160.4 287.2 all-reduce.2
where the time goes:
time: 463 us; the launch traced here: 456 us
  waiting for transfers between devices  266 us (57%)
  matrix products  91 us (20%)
  starting transfers between devices  37.1 us (8%)
  local copies, waits for them, and re-layouts  36.7 us (8%)
  between operations  15.5 us (3%)
  other arithmetic  10.2 us (2%)
    unnamed x2, waiting for transfers between devices  259 us
    dot_general x27, matrix products, convolve(): jnp.einsum('xyszc,dc->xyszd', sliced, kernel[offset], preferred_element_t...  30.5 us
    unnamed x80, local copies, waits for them, and re-layouts  29 us
    dot_general x27, matrix products, weight_terms(): jnp.einsum('xyszc,xyszd->cd', sliced, grads, preferred_element_type=jnp.f...  28.4 us
    ppermute x6, starting transfers between devices, with_halo(): before = lax.ppermute(last, axis, up)  27.4 us
    dot_general x27, matrix products, convolve(): jnp.einsum('xyszc,cd->xyszd', sliced, kernel[offset], preferred_element_t...  26.9 us
    ppermute x6, starting transfers between devices, with_halo(): after = lax.ppermute(leading, axis, down)  9.62 us
  transfers between devices with their start and end apart: 13, of which 4 were waited for; matrix products, arithmetic and copies ran while one was open for 5% of the time, Pallas kernels for 0%

commit v1 on v0

v1 whole, which is shorter than its diff:
```python
import functools
import math

import jax
import jax.numpy as jnp
from jax import lax
from jax.experimental import pallas as pl
from jax.experimental.pallas import tpu as pltpu
from jax.sharding import PartitionSpec as P

F32 = jnp.float32
BF16 = jnp.bfloat16
MESH = pl.DeviceIdType.MESH

DIRS = ((-1, 0), (1, 0), (0, -1), (0, 1), (-1, -1), (-1, 1), (1, -1), (1, 1))
COLS = (0, 8, 16, 24, 32, 33, 34, 35)
WIDE = (8, 8, 8, 8, 1, 1, 1, 1)
ENDS = (8, 15, 21, 27)
HALF = 216
PADDED = 224
UNIT = 32000.0


def up_down(v, top, bottom, z):
    rows = v.shape[0]
    lower = jnp.where(z == 0, bottom, pltpu.roll(v, 1, 0))
    higher = jnp.where(z == 15, top, pltpu.roll(v, rows - 1, 0))
    return lower, higher


def exponent(v):
    peak = jnp.max(jnp.abs(v), axis=0, keepdims=True)
    return jnp.ceil(jnp.log2(jnp.maximum(peak, 1e-30)))


def encode(v):
    k = exponent(v)
    q = jnp.floor(v * (jnp.exp2(-k) * UNIT) + 0.5)
    tail = jnp.broadcast_to(k, (PADDED - HALF, v.shape[1]))
    return jnp.concatenate([q, tail], axis=0).astype(jnp.int32).astype(jnp.int16)


def decode(q):
    w = q.astype(jnp.int32).astype(F32)
    return w[:HALF] * (jnp.exp2(w[HALF : HALF + 1]) * (1.0 / UNIT))


def kernel(
    scale, lev, cnt, f_hbm, g_hbm, w_hbm, out_ref, ig_ref, wg_ref,
    f_own, g_own, w_all, f_fr, g_fr, f_halo, g_halo, meta, near, ft, wg,
    r0, qx1, qy1, ownx, owny, rx1, ry1, qx2, qy2, rx2, ry2, total, q3, r3,
    load_sem, hs, hr, s0s, s0r, x1s, x1r, y1s, y1r, x2s, x2r, y2s, y2r, s3s, s3r,
):
    gx, gy = lax.axis_index("gx"), lax.axis_index("gy")
    y, xl, core = lax.div(gx, 4), lax.rem(lax.div(gx, 2), 2), lax.rem(gx, 2)
    z, xh = lax.div(gy, 2), lax.rem(gy, 2)
    x = xh * 2 + xl

    def place(y_, x_, core_, z_):
        return (y_ * 4 + lax.rem(x_, 2) * 2 + core_, z_ * 2 + lax.div(x_, 2))

    sibling = place(y, x, 1 - core, z)

    def x_peer(j):
        return lax.rem(x + j, 4)

    def y_peer(j):
        return lax.rem(y + j, 4)

    def neighbour(d):
        return (lax.rem(gx + d[0] + 16, 16), lax.rem(gy + d[1] + 16, 16))

    loads = [
        pltpu.make_async_copy(g_hbm, g_own, load_sem.at[0]),
        pltpu.make_async_copy(f_hbm, f_own, load_sem.at[1]),
        pltpu.make_async_copy(w_hbm, w_all, load_sem.at[2]),
    ]
    for c in loads:
        c.start()

    own_source = lax.div(z, 4) == xh
    barrier = pltpu.get_barrier_semaphore()
    for d in DIRS:
        pl.semaphore_signal(barrier, inc=1, device_id=neighbour(d), device_id_type=MESH)
    pl.semaphore_signal(barrier, inc=1, device_id=sibling, device_id_type=MESH)
    for j in (1, 2, 3):
        pl.semaphore_signal(barrier, inc=1, device_id=place(y, x_peer(j), core, z), device_id_type=MESH)
        pl.semaphore_signal(barrier, inc=1, device_id=place(y_peer(j), x, core, z), device_id_type=MESH)
    source_x = lax.div(z, 4) * 2 + xl
    for s in range(8):

        @pl.when(jnp.logical_not(jnp.logical_and(own_source, z == s)))
        def _():
            pl.semaphore_signal(barrier, inc=1, device_id=place(y, source_x, core, s), device_id_type=MESH)

    shift = lev[0, 0, 0].astype(F32)
    second = jnp.where(cnt[0, 0] >= 2, 1.0, 0.0).astype(F32)
    eight = lax.broadcasted_iota(jnp.int32, (8, 256), 0)
    meta[...] = jnp.where(eight < 4, shift, second)
    loads[0].wait()
    loads[1].wait()
    pl.semaphore_wait(barrier, 23 - own_source.astype(jnp.int32))

    def edge(ref, d):
        row = {-1: 0, 1: 7}
        if d[0] and d[1]:
            return ref.at[row[d[0]], row[d[1]]]
        return ref.at[row[d[0]]] if d[0] else ref.at[:, row[d[1]]]

    def slot(ref, i):
        return ref.at[COLS[i]] if WIDE[i] == 1 else ref.at[pl.ds(COLS[i], 8)]

    def halo(kind, i):
        d = DIRS[i]
        opposite = DIRS.index((-d[0], -d[1]))
        if kind == 0:
            src, dst = meta, near.at[opposite]
        else:
            src = edge((None, g_own, f_own)[kind], d)
            dst = slot((None, g_halo, f_halo)[kind], opposite)
        return pltpu.make_async_remote_copy(
            src_ref=src, dst_ref=dst, send_sem=hs.at[kind, i], recv_sem=hr.at[kind, opposite],
            device_id=neighbour(d), device_id_type=MESH,
        )

    started = []

    def go(copy):
        copy.start()
        started.append(copy)

    for kind in range(3):
        for i in range(8):
            go(halo(kind, i))

    def z_of(rows):
        return lax.rem(lax.broadcasted_iota(jnp.int32, (rows, 256), 0), 16)

    z128 = z_of(128)
    keep128 = jnp.where(z128 < 8, 1.0, second)

    def own_columns(src, fr, with_transpose):
        for r in range(8):
            v = src[r].reshape(128, 256).astype(F32) * keep128
            lower, higher = up_down(v, 0.0, 0.0, z128)
            for k, t in enumerate((lower, v, higher)):
                fr[k, r + 1, 1:9] = t.astype(BF16).reshape(8, 16, 256)
            if with_transpose:
                ft[:, r * 128 : (r + 1) * 128] = v.T.astype(BF16)

    own_columns(g_own, g_fr, False)
    own_columns(f_own, f_fr, True)

    def near_columns(kind, recv, fr):
        for i, (dx, dy) in enumerate(DIRS):
            if kind == 1:
                halo(0, DIRS.index((-dx, -dy))).wait_recv()
            halo(kind, DIRS.index((-dx, -dy))).wait_recv()
            n = WIDE[i]
            inside = jnp.logical_and(
                jnp.logical_and(gx + dx >= 0, gx + dx < 16), jnp.logical_and(gy + dy >= 0, gy + dy < 16)
            )
            valid = jnp.where(inside, 1.0, 0.0).astype(F32)
            higher_by = near[i, 0:1, :] - shift
            level = jnp.where(higher_by == 0.0, valid, 0.0)
            above = jnp.where(higher_by == 1.0, valid, 0.0)
            below = jnp.where(higher_by == -1.0, valid, 0.0)
            rows = n * 16
            zr = z_of(rows)
            v = recv[COLS[i] : COLS[i] + n].reshape(rows, 256).astype(F32)
            v = v * jnp.where(zr < 8, 1.0, near[i, 4:5, :])
            swapped = pltpu.roll(v, 8, 0) if n == 1 else None
            up8 = swapped if n == 1 else pltpu.roll(v, 8, 0)
            down8 = swapped if n == 1 else pltpu.roll(v, rows - 8, 0)
            c = level * v + jnp.where(zr >= 8, above * up8, below * down8)
            top = above * pltpu.roll(v, 7, 0)
            bottom = below * pltpu.roll(v, rows - 7, 0)
            lower, higher = up_down(c, top, bottom, zr)
            xs = {-1: 0, 0: slice(1, 9), 1: 9}[dx]
            ys = {-1: 0, 0: slice(1, 9), 1: 9}[dy]
            for k, t in enumerate((lower, c, higher)):
                t = t.astype(BF16)
                fr[k, xs, ys] = t if n == 1 else t.reshape(8, 16, 256)

    near_columns(1, g_halo, g_fr)

    first = y_peer(1)
    base = lax.div(27 * first, 4)

    def gradient(i):
        o = lax.rem(base + i, 27)
        dx, dy, dz = lax.div(o, 9), lax.rem(lax.div(o, 3), 3), lax.rem(o, 3)
        g = g_fr[2 - dz, pl.ds(2 - dx, 8), pl.ds(2 - dy, 8)].reshape(1024, 256)
        wg[pl.ds(pl.multiple_of(o * 256, 256), 256), :] = jnp.dot(ft[...], g, preferred_element_type=F32)

    def phase_y(p):
        return lax.rem(y + 1 + p, 4)

    def rows_of(p, xl_, core_):
        return pl.multiple_of(((phase_y(p) * 2 + xl_) * 2 + core_) * (2 * HALF), 8)

    def send0(p):
        for a in range(2):
            go(pltpu.make_async_remote_copy(
                src_ref=wg.at[pl.ds(rows_of(p, a, 1 - core), 2 * HALF)], dst_ref=r0.at[p, a],
                send_sem=s0s.at[p, a], recv_sem=s0r.at[p, a], device_id=sibling, device_id_type=MESH,
            ))

    def copy_x1(p, j):
        return pltpu.make_async_remote_copy(
            src_ref=qx1.at[p, j - 1], dst_ref=rx1.at[p, j - 1], send_sem=x1s.at[p, j - 1],
            recv_sem=x1r.at[p, j - 1], device_id=place(y, x_peer(j), core, z), device_id_type=MESH,
        )

    def copy_y1(p):
        return pltpu.make_async_remote_copy(
            src_ref=qy1.at[p], dst_ref=ry1.at[p], send_sem=y1s.at[p], recv_sem=y1r.at[p],
            device_id=place(phase_y(p), x, core, z), device_id_type=MESH,
        )

    def send1(p):
        for a in range(2):
            pltpu.make_async_remote_copy(
                src_ref=wg.at[pl.ds(rows_of(p, a, 1 - core), 2 * HALF)], dst_ref=r0.at[p, a],
                send_sem=s0s.at[p, a], recv_sem=s0r.at[p, a], device_id=sibling, device_id_type=MESH,
            ).wait_recv()
        for a in range(2):
            for h in range(2):
                mine = wg[pl.ds(pl.multiple_of(rows_of(p, a, core) + h * HALF, 8), HALF), 128:256]
                v = mine + r0[p, a, h * HALF : (h + 1) * HALF, 128:256]
                if p < 3:
                    qy1[p, a * 2 + h] = encode(v)
                else:
                    owny[a * 2 + h] = v
        if p < 3:
            go(copy_y1(p))
        for j in (2, 1, 3, 0):
            to = x_peer(j)
            a, h = lax.rem(to, 2), lax.div(to, 2)
            mine = wg[pl.ds(pl.multiple_of(rows_of(p, a, core) + h * HALF, 8), HALF), 0:128]
            v = mine + r0[p, a, pl.ds(pl.multiple_of(h * HALF, 8), HALF), 0:128]
            if j:
                qx1[p, j - 1] = encode(v)
                go(copy_x1(p, j))
            else:
                ownx[p] = v

    def copy_x2(p):
        return pltpu.make_async_remote_copy(
            src_ref=qx2.at[p], dst_ref=rx2.at[p], send_sem=x2s.at[p], recv_sem=x2r.at[p],
            device_id=place(phase_y(p), x, core, z), device_id_type=MESH,
        )

    def copy_y2(j):
        return pltpu.make_async_remote_copy(
            src_ref=qy2.at[j - 1], dst_ref=ry2.at[j - 1], send_sem=y2s.at[j - 1], recv_sem=y2r.at[j - 1],
            device_id=place(y, x_peer(j), core, z), device_id_type=MESH,
        )

    def send2x(p):
        v = ownx[p]
        for j in (1, 2, 3):
            copy_x1(p, j).wait_recv()
            v = v + decode(rx1[p, j - 1])
        if p < 3:
            qx2[p] = encode(v)
            go(copy_x2(p))
        else:
            total[0:HALF, 0:128] = v

    def send2y():
        for p in range(3):
            copy_y1(p).wait_recv()
        for j in (2, 1, 3, 0):
            to = x_peer(j)
            i = lax.rem(to, 2) * 2 + lax.div(to, 2)
            v = owny[i]
            for p in range(3):
                v = v + decode(ry1[p, i])
            if j:
                qy2[j - 1] = encode(v)
                go(copy_y2(j))
            else:
                total[0:HALF, 128:256] = v

    row32 = lax.broadcasted_iota(jnp.int32, (32, 256), 0)

    def copy_3(j):
        return pltpu.make_async_remote_copy(
            src_ref=q3.at[j], dst_ref=r3.at[z], send_sem=s3s.at[j], recv_sem=s3r.at[z],
            device_id=place(y, (j % 2) * 2 + xl, core, xh * 4 + j // 2), device_id_type=MESH,
        )

    def is_self(j):
        return jnp.logical_and(own_source, lax.rem(z, 4) * 2 + xh == j)

    def send3():
        v = total[0:HALF, 0:128]
        for p in range(3):
            copy_x2(p).wait_recv()
            v = v + decode(rx2[p])
        total[0:HALF, 0:128] = v
        v = total[0:HALF, 128:256]
        for j in (1, 2, 3):
            copy_y2(j).wait_recv()
            v = v + decode(ry2[j - 1])
        total[0:HALF, 128:256] = v
        total[HALF:PADDED, :] = jnp.zeros((PADDED - HALF, 256), F32)
        for j in range(8):
            v = jnp.where(row32 < 27, total[27 * j : 27 * j + 32, :], 0.0)
            k = exponent(v)
            q = jnp.floor(v * (jnp.exp2(-k) * UNIT) + 0.5)
            q3[j] = jnp.where(row32 < 27, q, k).astype(jnp.int32).astype(jnp.int16)

            @pl.when(jnp.logical_not(is_self(j)))
            def _():
                copy_3(j).start()

            @pl.when(is_self(j))
            def _():
                r3[z] = q3[j]

    def finish():
        v = jnp.zeros((32, 256), F32)
        for s in range(8):

            @pl.when(jnp.logical_not(jnp.logical_and(own_source, z == s)))
            def _():
                pltpu.make_async_remote_copy(
                    src_ref=q3.at[s], dst_ref=r3.at[s], send_sem=s3s.at[s], recv_sem=s3r.at[s],
                    device_id=place(y, source_x, core, s), device_id_type=MESH,
                ).wait_recv()

            w = r3[s].astype(jnp.int32).astype(F32)
            v = v + w * (jnp.exp2(w[31:32]) * (1.0 / UNIT))
        wg_ref[...] = (v * scale)[:27]

    keep256 = jnp.where(z_of(256) < 8, 1.0, second)

    def convolve(fr, dst, transposed, lo, hi):
        def tile(t, _):
            acc = None
            for o in range(27):
                dx, dy, dz = o // 9, o // 3 % 3, o % 3
                a = fr[dz, pl.ds(2 * t + dx, 2), pl.ds(dy, 8)].reshape(256, 256)
                if transposed:
                    term = lax.dot_general(
                        a, w_all[26 - o], (((1,), (1,)), ((), ())), preferred_element_type=F32
                    )
                else:
                    term = jnp.dot(a, w_all[o], preferred_element_type=F32)
                acc = term if acc is None else acc + term
            dst[pl.ds(2 * t, 2)] = (acc * keep256).astype(BF16).reshape(2, 8, 16, 256)
            return 0

        lax.fori_loop(lo, hi, tile, 0)

    done = 0
    for p in range(4):
        for i in range(done, ENDS[p]):
            gradient(i)
        done = ENDS[p]
        send0(p)
        if p:
            send1(p - 1)
    near_columns(2, f_halo, f_fr)
    loads[2].wait()
    convolve(f_fr, out_ref, False, 0, 1)
    send1(3)
    convolve(f_fr, out_ref, False, 1, 4)
    send2x(0)
    send2x(1)
    convolve(g_fr, ig_ref, True, 0, 2)
    send2x(2)
    send2y()
    send2x(3)
    convolve(g_fr, ig_ref, True, 2, 4)
    send3()
    finish()
    for c in started:
        c.wait_send()
    for j in range(8):

        @pl.when(jnp.logical_not(is_self(j)))
        def _():
            copy_3(j).wait_send()


def per_device(features, cotangent, weights, levels, counts):
    f = features.reshape(8, 8, 16, 256)
    g = cotangent.reshape(8, 8, 16, 256)
    scale = 1.0 / math.sqrt(1024 * lax.axis_size("gx") * lax.axis_size("gy"))
    vmem = pl.BlockSpec(memory_space=pltpu.VMEM)
    smem = pl.BlockSpec(memory_space=pltpu.SMEM)
    anywhere = pl.BlockSpec(memory_space=pl.ANY)
    dma = pltpu.SemaphoreType.DMA
    i16 = jnp.int16
    out, ig, wgrad = pl.pallas_call(
        functools.partial(kernel, scale),
        out_shape=(
            jax.ShapeDtypeStruct((8, 8, 16, 256), BF16),
            jax.ShapeDtypeStruct((8, 8, 16, 256), BF16),
            jax.ShapeDtypeStruct((27, 256), F32),
        ),
        in_specs=[smem, smem, anywhere, anywhere, anywhere],
        out_specs=(vmem, vmem, vmem),
        scratch_shapes=[
            pltpu.VMEM((8, 8, 16, 256), BF16),
            pltpu.VMEM((8, 8, 16, 256), BF16),
            pltpu.VMEM((27, 256, 256), BF16),
            pltpu.VMEM((3, 10, 10, 16, 256), BF16),
            pltpu.VMEM((3, 10, 10, 16, 256), BF16),
            pltpu.VMEM((36, 16, 256), BF16),
            pltpu.VMEM((36, 16, 256), BF16),
            pltpu.VMEM((8, 256), F32),
            pltpu.VMEM((8, 8, 256), F32),
            pltpu.VMEM((256, 1024), BF16),
            pltpu.VMEM((6912, 256), F32),
            pltpu.VMEM((4, 2, 2 * HALF, 256), F32),
            pltpu.VMEM((4, 3, PADDED, 128), i16),
            pltpu.VMEM((3, 4, PADDED, 128), i16),
            pltpu.VMEM((4, HALF, 128), F32),
            pltpu.VMEM((4, HALF, 128), F32),
            pltpu.VMEM((4, 3, PADDED, 128), i16),
            pltpu.VMEM((3, 4, PADDED, 128), i16),
            pltpu.VMEM((3, PADDED, 128), i16),
            pltpu.VMEM((3, PADDED, 128), i16),
            pltpu.VMEM((3, PADDED, 128), i16),
            pltpu.VMEM((3, PADDED, 128), i16),
            pltpu.VMEM((PADDED, 256), F32),
            pltpu.VMEM((8, 32, 256), i16),
            pltpu.VMEM((8, 32, 256), i16),
            dma((3,)),
            dma((3, 8)),
            dma((3, 8)),
            dma((4, 2)),
            dma((4, 2)),
            dma((4, 3)),
            dma((4, 3)),
            dma((3,)),
            dma((3,)),
            dma((3,)),
            dma((3,)),
            dma((3,)),
            dma((3,)),
            dma((8,)),
            dma((8,)),
        ],
        compiler_params=pltpu.CompilerParams(
            collective_id=0, has_side_effects=True, vmem_limit_bytes=56 * 1024 * 1024
        ),
    )(levels, counts, f, g, weights)
    shape = features.shape
    return out.reshape(shape), ig.reshape(shape), wgrad.reshape(-1)


def solution(mesh):
    return jax.shard_map(
        per_device,
        mesh=mesh,
        in_specs=(
            P("gx", "gy", None, None, None),
            P("gx", "gy", None, None, None),
            P(),
            P("gx", "gy", None),
            P("gx", "gy"),
        ),
        out_specs=(
            P("gx", "gy", None, None, None),
            P("gx", "gy", None, None, None),
            P(("gx", "gy")),
        ),
        check_vma=False,
    )
```

time: 463 us -> 59.9 us (0.13); the launches traced: 456 us -> 59 us
  waiting for transfers between devices: 266 us -> 0 us
  matrix products: 91 us -> 0 us
  Pallas kernels: 0 us -> 52.6 us
  starting transfers between devices: 37.1 us -> 0 us
  local copies, waits for them, and re-layouts: 36.7 us -> 5.1 us
  between operations: 15.5 us -> 1.29 us
  other arithmetic: 10.2 us -> 0 us
    unnamed x2 -> x0, waiting for transfers between devices: 259 us -> none
    dot_general x83 -> x0, matrix products: 91 us -> none  [the longest x27 30.5 us: convolve(): jnp.einsum('xyszc,dc->xyszd', sliced, kernel[offset], preferred_element_t...]
    pallas_call x0 -> x1, Pallas kernels: none -> 52.6 us  [per_device(): pl.pallas_call(functools.partial(kernel, scale), out_shape=(jax.ShapeDtyp...]
    ppermute x12 -> x0, starting transfers between devices: 37.1 us -> none  [the longest x6 27.4 us: with_halo(): before = lax.ppermute(last, axis, up)]
    unnamed x80 -> x2, local copies, waits for them, and re-layouts: 29 us -> 3.73 us
    ppermute x12 -> x0, waiting for transfers between devices: 6.18 us -> none  [the longest x6 5.44 us: with_halo(): after = lax.ppermute(leading, axis, down)]
    concatenate x5 -> x0, other arithmetic: 5.56 us -> none  [the longest x2 5.26 us: assemble(): jnp.concatenate([below_layer, same_level, above_layer], axis=3)]
    slice x6 -> x0, local copies, waits for them, and re-layouts: 5.33 us -> none  [the longest x2 3.97 us: assemble(): same_level = stacked[:, :, :, 1]]
  transfers between devices with their start and end apart: 13 -> 0, of which waited for: 4 -> 0; matrix products, arithmetic and copies ran while one was open for 5% -> 0% of each run, Pallas kernels for 0% -> 0%
where the time goes in v1:
time: 59.9 us; the launch traced here: 59 us
  Pallas kernels  52.6 us (88%)
  local copies, waits for them, and re-layouts  5.1 us (9%)
  between operations  1.29 us (2%)
    pallas_call x1, Pallas kernels, per_device(): pl.pallas_call(functools.partial(kernel, scale), out_shape=(jax.ShapeDtyp...  52.6 us
    unnamed x2, local copies, waits for them, and re-layouts  3.73 us
    reshape x1, local copies, waits for them, and re-layouts, per_device(): return (out.reshape(shape), ig.reshape(shape), wgrad.reshape(-1))  1.37 us

profile of v1, /device:TPU:1, one launch (start us, length us, event | category | flops | bytes accessed | tf_op | source)
XLA Modules:
  0.0 59.0 jit_solution(10405359245328158211)
XLA Ops:
  1.3 52.6 %shard_map.76 = (bf16[8,8,16,256]{3,2,1,0:T(8,128)(2,1)}, bf16[8,8,16,256]{3,2,1,0:T(8,128)(2,1)}, f32[27,256]{1,0:T(8,128)}) custom-call(s32[1,1,2]{2,1,0:T(1,128)} %lev.1, s32[1,1]{1,0:T(1,128)S(6)} %copy.10.cnt, bf16[8,8,16,256]{3,2,1,0:T(8,128)(2,1)} %bitcast.4, bf16[8,8,16,256]{3,2,1,0:T(8,128)(2,1)} %bitcast.5, bf16[27,256,256]{2,1,0:T(8,128)(2,1)} %w_hbm.1), custom_call_target="tpu_custom_call" | custom-call | tf_op jit(solution)/shard_map/pallas_call | solution.py:398
  53.9 1.4 %reshape.25 = f32[6912]{0:T(1024)} reshape(f32[27,256]{1,0:T(8,128)} %get-tuple-element.8) | data formatting | bytes 55296 | tf_op jit(solution)/shard_map/reshape | solution.py:454
  55.3 1.9 %copy.11 = bf16[8,8,2,8,256]{4,3,2,1,0:T(8,128)(2,1)} copy(bf16[8,8,2,8,256]{4,3,2,1,0:T(8,128)(2,1)} %bitcast.7) | data formatting | bytes 1048576
  57.2 1.9 %copy.12 = bf16[8,8,2,8,256]{4,3,2,1,0:T(8,128)(2,1)} copy(bf16[8,8,2,8,256]{4,3,2,1,0:T(8,128)(2,1)} %bitcast.6) | data formatting | bytes 1048576

commit v2 on v1

--- a/solution.py
+++ b/solution.py
@@ -15,8 +15,10 @@
 DIRS = ((-1, 0), (1, 0), (0, -1), (0, 1), (-1, -1), (-1, 1), (1, -1), (1, 1))
 COLS = (0, 8, 16, 24, 32, 33, 34, 35)
 WIDE = (8, 8, 8, 8, 1, 1, 1, 1)
-ENDS = (8, 15, 21, 27)
-HALF = 216
+PHASES = tuple((p, a) for p in range(4) for a in range(2))
+ENDS = (5, 8, 11, 15, 18, 21, 25, 27)
+SHARE = 27
+HALF = 8 * SHARE
 PADDED = 224
 UNIT = 32000.0
 
@@ -48,7 +50,7 @@
 def kernel(
     scale, lev, cnt, f_hbm, g_hbm, w_hbm, out_ref, ig_ref, wg_ref,
     f_own, g_own, w_all, f_fr, g_fr, f_halo, g_halo, meta, near, ft, wg,
-    r0, qx1, qy1, ownx, owny, rx1, ry1, qx2, qy2, rx2, ry2, total, q3, r3,
+    r0, pair, parted, qx1, qy1, ownx, owny, rx1, ry1, qx2, qy2, rx2, ry2, total, q3, r3,
     load_sem, hs, hr, s0s, s0r, x1s, x1r, y1s, y1r, x2s, x2r, y2s, y2r, s3s, s3r,
 ):
     gx, gy = lax.axis_index("gx"), lax.axis_index("gy")
@@ -66,6 +68,9 @@
 
     def y_peer(j):
         return lax.rem(y + j, 4)
+
+    def z_peer(j):
+        return lax.rem(z + j, 8)
 
     def neighbour(d):
         return (lax.rem(gx + d[0] + 16, 16), lax.rem(gy + d[1] + 16, 16))
@@ -78,7 +83,6 @@
     for c in loads:
         c.start()
 
-    own_source = lax.div(z, 4) == xh
     barrier = pltpu.get_barrier_semaphore()
     for d in DIRS:
         pl.semaphore_signal(barrier, inc=1, device_id=neighbour(d), device_id_type=MESH)
@@ -86,12 +90,8 @@
     for j in (1, 2, 3):
         pl.semaphore_signal(barrier, inc=1, device_id=place(y, x_peer(j), core, z), device_id_type=MESH)
         pl.semaphore_signal(barrier, inc=1, device_id=place(y_peer(j), x, core, z), device_id_type=MESH)
-    source_x = lax.div(z, 4) * 2 + xl
-    for s in range(8):
-
-        @pl.when(jnp.logical_not(jnp.logical_and(own_source, z == s)))
-        def _():
-            pl.semaphore_signal(barrier, inc=1, device_id=place(y, source_x, core, s), device_id_type=MESH)
+    for j in range(1, 8):
+        pl.semaphore_signal(barrier, inc=1, device_id=place(y, x, core, z_peer(j)), device_id_type=MESH)
 
     shift = lev[0, 0, 0].astype(F32)
     second = jnp.where(cnt[0, 0] >= 2, 1.0, 0.0).astype(F32)
@@ -99,7 +99,7 @@
     meta[...] = jnp.where(eight < 4, shift, second)
     loads[0].wait()
     loads[1].wait()
-    pl.semaphore_wait(barrier, 23 - own_source.astype(jnp.int32))
+    pl.semaphore_wait(barrier, 22)
 
     def edge(ref, d):
         row = {-1: 0, 1: 7}
@@ -129,7 +129,7 @@
         copy.start()
         started.append(copy)
 
-    for kind in range(3):
+    for kind in range(2):
         for i in range(8):
             go(halo(kind, i))
 
@@ -183,6 +183,8 @@
                 fr[k, xs, ys] = t if n == 1 else t.reshape(8, 16, 256)
 
     near_columns(1, g_halo, g_fr)
+    for i in range(8):
+        go(halo(2, i))
 
     first = y_peer(1)
     base = lax.div(27 * first, 4)
@@ -199,12 +201,11 @@
     def rows_of(p, xl_, core_):
         return pl.multiple_of(((phase_y(p) * 2 + xl_) * 2 + core_) * (2 * HALF), 8)
 
-    def send0(p):
-        for a in range(2):
-            go(pltpu.make_async_remote_copy(
-                src_ref=wg.at[pl.ds(rows_of(p, a, 1 - core), 2 * HALF)], dst_ref=r0.at[p, a],
-                send_sem=s0s.at[p, a], recv_sem=s0r.at[p, a], device_id=sibling, device_id_type=MESH,
-            ))
+    def copy_0(p, a):
+        return pltpu.make_async_remote_copy(
+            src_ref=wg.at[pl.ds(rows_of(p, a, 1 - core), 2 * HALF)], dst_ref=r0.at[p, a],
+            send_sem=s0s.at[p, a], recv_sem=s0r.at[p, a], device_id=sibling, device_id_type=MESH,
+        )
 
     def copy_x1(p, j):
         return pltpu.make_async_remote_copy(
@@ -212,38 +213,41 @@
             recv_sem=x1r.at[p, j - 1], device_id=place(y, x_peer(j), core, z), device_id_type=MESH,
         )
 
-    def copy_y1(p):
-        return pltpu.make_async_remote_copy(
-            src_ref=qy1.at[p], dst_ref=ry1.at[p], send_sem=y1s.at[p], recv_sem=y1r.at[p],
+    def copy_y1(p, a):
+        return pltpu.make_async_remote_copy(
+            src_ref=qy1.at[p, a], dst_ref=ry1.at[p, a], send_sem=y1s.at[p, a], recv_sem=y1r.at[p, a],
             device_id=place(phase_y(p), x, core, z), device_id_type=MESH,
         )
 
-    def send1(p):
-        for a in range(2):
-            pltpu.make_async_remote_copy(
-                src_ref=wg.at[pl.ds(rows_of(p, a, 1 - core), 2 * HALF)], dst_ref=r0.at[p, a],
-                send_sem=s0s.at[p, a], recv_sem=s0r.at[p, a], device_id=sibling, device_id_type=MESH,
-            ).wait_recv()
-        for a in range(2):
-            for h in range(2):
-                mine = wg[pl.ds(pl.multiple_of(rows_of(p, a, core) + h * HALF, 8), HALF), 128:256]
-                v = mine + r0[p, a, h * HALF : (h + 1) * HALF, 128:256]
-                if p < 3:
-                    qy1[p, a * 2 + h] = encode(v)
-                else:
-                    owny[a * 2 + h] = v
+    def steps_to(h, a):
+        return lax.rem(h * 2 + a - x + 4, 4)
+
+    def send1(p, a):
+        copy_0(p, a).wait_recv()
+        pair[...] = wg[pl.ds(rows_of(p, a, core), 2 * HALF), :] + r0[p, a]
+        for h in range(2):
+            for k in range(8):
+                parted[h, SHARE * k : SHARE * (k + 1), :] = pair[SHARE * (2 * k + h) : SHARE * (2 * k + h + 1), :]
+        for h in range(2):
+            j = steps_to(h, a)
+            coded = encode(parted[h, :, 0:128])
+
+            @pl.when(j != 0)
+            def _():
+                qx1[p, j - 1] = coded
+                copy_x1(p, j).start()
+
+            @pl.when(j == 0)
+            def _():
+                ownx[p] = parted[h, :, 0:128]
+
+        for h in range(2):
+            if p < 3:
+                qy1[p, a, h] = encode(parted[h, :, 128:256])
+            else:
+                owny[a, h] = parted[h, :, 128:256]
         if p < 3:
-            go(copy_y1(p))
-        for j in (2, 1, 3, 0):
-            to = x_peer(j)
-            a, h = lax.rem(to, 2), lax.div(to, 2)
-            mine = wg[pl.ds(pl.multiple_of(rows_of(p, a, core) + h * HALF, 8), HALF), 0:128]
-            v = mine + r0[p, a, pl.ds(pl.multiple_of(h * HALF, 8), HALF), 0:128]
-            if j:
-                qx1[p, j - 1] = encode(v)
-                go(copy_x1(p, j))
-            else:
-                ownx[p] = v
+            go(copy_y1(p, a))
 
     def copy_x2(p):
         return pltpu.make_async_remote_copy(
@@ -259,7 +263,7 @@
 
     def send2x(p):
         v = ownx[p]
-        for j in (1, 2, 3):
+        for j in (1, 3, 2):
             copy_x1(p, j).wait_recv()
             v = v + decode(rx1[p, j - 1])
         if p < 3:
@@ -268,31 +272,32 @@
         else:
             total[0:HALF, 0:128] = v
 
-    def send2y():
+    def send2y(a):
         for p in range(3):
-            copy_y1(p).wait_recv()
-        for j in (2, 1, 3, 0):
-            to = x_peer(j)
-            i = lax.rem(to, 2) * 2 + lax.div(to, 2)
-            v = owny[i]
+            copy_y1(p, a).wait_recv()
+        for h in range(2):
+            j = steps_to(h, a)
+            v = owny[a, h]
             for p in range(3):
-                v = v + decode(ry1[p, i])
-            if j:
-                qy2[j - 1] = encode(v)
-                go(copy_y2(j))
-            else:
+                v = v + decode(ry1[p, a, h])
+            coded = encode(v)
+
+            @pl.when(j != 0)
+            def _():
+                qy2[j - 1] = coded
+                copy_y2(j).start()
+
+            @pl.when(j == 0)
+            def _():
                 total[0:HALF, 128:256] = v
 
     row32 = lax.broadcasted_iota(jnp.int32, (32, 256), 0)
 
     def copy_3(j):
         return pltpu.make_async_remote_copy(
-            src_ref=q3.at[j], dst_ref=r3.at[z], send_sem=s3s.at[j], recv_sem=s3r.at[z],
-            device_id=place(y, (j % 2) * 2 + xl, core, xh * 4 + j // 2), device_id_type=MESH,
-        )
-
-    def is_self(j):
-        return jnp.logical_and(own_source, lax.rem(z, 4) * 2 + xh == j)
+            src_ref=q3.at[z_peer(j)], dst_ref=r3.at[j - 1], send_sem=s3s.at[j - 1], recv_sem=s3r.at[j - 1],
+            device_id=place(y, x, core, z_peer(j)), device_id_type=MESH,
+        )
 
     def send3():
         v = total[0:HALF, 0:128]
@@ -306,34 +311,26 @@
             v = v + decode(ry2[j - 1])
         total[0:HALF, 128:256] = v
         total[HALF:PADDED, :] = jnp.zeros((PADDED - HALF, 256), F32)
-        for j in range(8):
-            v = jnp.where(row32 < 27, total[27 * j : 27 * j + 32, :], 0.0)
+        for s in range(8):
+            v = jnp.where(row32 < SHARE, total[SHARE * s : SHARE * s + 32, :], 0.0)
             k = exponent(v)
             q = jnp.floor(v * (jnp.exp2(-k) * UNIT) + 0.5)
-            q3[j] = jnp.where(row32 < 27, q, k).astype(jnp.int32).astype(jnp.int16)
-
-            @pl.when(jnp.logical_not(is_self(j)))
-            def _():
-                copy_3(j).start()
-
-            @pl.when(is_self(j))
-            def _():
-                r3[z] = q3[j]
+            q3[s] = jnp.where(row32 < SHARE, q, k).astype(jnp.int32).astype(jnp.int16)
+        for j in (4, 3, 5, 2, 6, 1, 7):
+            go(copy_3(j))
 
     def finish():
-        v = jnp.zeros((32, 256), F32)
-        for s in range(8):
-
-            @pl.when(jnp.logical_not(jnp.logical_and(own_source, z == s)))
-            def _():
-                pltpu.make_async_remote_copy(
-                    src_ref=q3.at[s], dst_ref=r3.at[s], send_sem=s3s.at[s], recv_sem=s3r.at[s],
-                    device_id=place(y, source_x, core, s), device_id_type=MESH,
-                ).wait_recv()
-
-            w = r3[s].astype(jnp.int32).astype(F32)
-            v = v + w * (jnp.exp2(w[31:32]) * (1.0 / UNIT))
-        wg_ref[...] = (v * scale)[:27]
+        def value(q):
+            w = q.astype(jnp.int32).astype(F32)
+            return w * (jnp.exp2(w[31:32]) * (1.0 / UNIT))
+
+        v = value(q3[z])
+        for j in (1, 7, 2, 6, 3, 5, 4):
+            copy_3(j).wait_recv()
+            v = v + value(r3[j - 1])
+        v = v * scale
+        wg_ref[pl.ds(0, SHARE, stride=2), :] = v[:SHARE, 0:128]
+        wg_ref[pl.ds(1, SHARE, stride=2), :] = v[:SHARE, 128:256]
 
     keep256 = jnp.where(z_of(256) < 8, 1.0, second)
 
@@ -356,34 +353,51 @@
         lax.fori_loop(lo, hi, tile, 0)
 
     done = 0
-    for p in range(4):
-        for i in range(done, ENDS[p]):
+    for n, (p, a) in enumerate(PHASES):
+        for i in range(done, ENDS[n]):
             gradient(i)
-        done = ENDS[p]
-        send0(p)
-        if p:
-            send1(p - 1)
-    near_columns(2, f_halo, f_fr)
+        done = ENDS[n]
+        copy_0(p, a).start()
+        if n >= 2:
+            send1(*PHASES[n - 2])
+    send1(*PHASES[6])
     loads[2].wait()
-    convolve(f_fr, out_ref, False, 0, 1)
-    send1(3)
-    convolve(f_fr, out_ref, False, 1, 4)
+    convolve(g_fr, ig_ref, True, 0, 1)
+    send1(*PHASES[7])
+    convolve(g_fr, ig_ref, True, 1, 4)
     send2x(0)
     send2x(1)
-    convolve(g_fr, ig_ref, True, 0, 2)
+    send2y(0)
+    send2y(1)
     send2x(2)
-    send2y()
     send2x(3)
-    convolve(g_fr, ig_ref, True, 2, 4)
     send3()
+    near_columns(2, f_halo, f_fr)
+    convolve(f_fr, out_ref, False, 0, 4)
     finish()
     for c in started:
         c.wait_send()
-    for j in range(8):
-
-        @pl.when(jnp.logical_not(is_self(j)))
-        def _():
-            copy_3(j).wait_send()
+    for p, a in PHASES:
+        copy_0(p, a).wait_send()
+    for j in (1, 2, 3):
+        for p in range(4):
+            copy_x1(p, j).wait_send()
+        copy_y2(j).wait_send()
+
+
+def hand_over(a, b, c, a_out, b_out, c_out, a_buf, b_buf, c_buf, in_sems, out_sems):
+    moves = [(a, a_buf, a_out, pl.ds(2 * i, 2)) for i in range(4)]
+    moves += [(b, b_buf, b_out, pl.ds(2 * i, 2)) for i in range(4)]
+    moves += [(c, c_buf, c_out, pl.ds(0, 2 * SHARE))]
+    ins = [pltpu.make_async_copy(v.at[part], buf.at[part], in_sems.at[i]) for i, (v, buf, _, part) in enumerate(moves)]
+    outs = [pltpu.make_async_copy(buf.at[part], o.at[part], out_sems.at[i]) for i, (_, buf, o, part) in enumerate(moves)]
+    for copy in ins:
+        copy.start()
+    for copy_in, copy_out in zip(ins, outs):
+        copy_in.wait()
+        copy_out.start()
+    for copy in outs:
+        copy.wait()
 
 
 def per_device(features, cotangent, weights, levels, counts):
@@ -400,7 +414,7 @@
         out_shape=(
             jax.ShapeDtypeStruct((8, 8, 16, 256), BF16),
             jax.ShapeDtypeStruct((8, 8, 16, 256), BF16),
-            jax.ShapeDtypeStruct((27, 256), F32),
+            jax.ShapeDtypeStruct((2 * SHARE, 128), F32),
         ),
         in_specs=[smem, smem, anywhere, anywhere, anywhere],
         out_specs=(vmem, vmem, vmem),
@@ -417,19 +431,21 @@
             pltpu.VMEM((256, 1024), BF16),
             pltpu.VMEM((6912, 256), F32),
             pltpu.VMEM((4, 2, 2 * HALF, 256), F32),
+            pltpu.VMEM((2 * HALF, 256), F32),
+            pltpu.VMEM((2, HALF, 256), F32),
             pltpu.VMEM((4, 3, PADDED, 128), i16),
-            pltpu.VMEM((3, 4, PADDED, 128), i16),
+            pltpu.VMEM((3, 2, 2, PADDED, 128), i16),
             pltpu.VMEM((4, HALF, 128), F32),
-            pltpu.VMEM((4, HALF, 128), F32),
+            pltpu.VMEM((2, 2, HALF, 128), F32),
             pltpu.VMEM((4, 3, PADDED, 128), i16),
-            pltpu.VMEM((3, 4, PADDED, 128), i16),
+            pltpu.VMEM((3, 2, 2, PADDED, 128), i16),
             pltpu.VMEM((3, PADDED, 128), i16),
             pltpu.VMEM((3, PADDED, 128), i16),
             pltpu.VMEM((3, PADDED, 128), i16),
             pltpu.VMEM((3, PADDED, 128), i16),
             pltpu.VMEM((PADDED, 256), F32),
             pltpu.VMEM((8, 32, 256), i16),
-            pltpu.VMEM((8, 32, 256), i16),
+            pltpu.VMEM((7, 32, 256), i16),
             dma((3,)),
             dma((3, 8)),
             dma((3, 8)),
@@ -437,19 +453,32 @@
             dma((4, 2)),
             dma((4, 3)),
             dma((4, 3)),
+            dma((3, 2)),
+            dma((3, 2)),
             dma((3,)),
             dma((3,)),
             dma((3,)),
             dma((3,)),
-            dma((3,)),
-            dma((3,)),
-            dma((8,)),
-            dma((8,)),
+            dma((7,)),
+            dma((7,)),
         ],
         compiler_params=pltpu.CompilerParams(
             collective_id=0, has_side_effects=True, vmem_limit_bytes=56 * 1024 * 1024
         ),
     )(levels, counts, f, g, weights)
+    out, ig, wgrad = pl.pallas_call(
+        hand_over,
+        out_shape=tuple(jax.ShapeDtypeStruct(v.shape, v.dtype) for v in (out, ig, wgrad)),
+        in_specs=[anywhere] * 3,
+        out_specs=(anywhere,) * 3,
+        scratch_shapes=[
+            pltpu.VMEM(out.shape, BF16),
+            pltpu.VMEM(ig.shape, BF16),
+            pltpu.VMEM(wgrad.shape, F32),
+            dma((9,)),
+            dma((9,)),
+        ],
+    )(out, ig, wgrad)
     shape = features.shape
     return out.reshape(shape), ig.reshape(shape), wgrad.reshape(-1)
 

time: 59.9 us -> 51.2 us (0.85); the launches traced: 59 us -> 51.1 us
  local copies, waits for them, and re-layouts: 5.1 us -> 0 us
  Pallas kernels: 52.6 us -> 49.8 us
    pallas_call x1, Pallas kernels: 52.6 us -> 47.7 us  [per_device(): pl.pallas_call(functools.partial(kernel, scale), out_shape=(jax.ShapeDtyp...]
    unnamed x2 -> x0, local copies, waits for them, and re-layouts: 3.73 us -> none
    pallas_call x0 -> x1, Pallas kernels: none -> 2.11 us  [per_device(): pl.pallas_call(hand_over, out_shape=tuple((jax.ShapeDtypeStruct(v.shape,...]
    reshape x1 -> x0, local copies, waits for them, and re-layouts: 1.37 us -> none  [per_device(): return (out.reshape(shape), ig.reshape(shape), wgrad.reshape(-1))]
where the time goes in v2:
time: 51.2 us; the launch traced here: 51.1 us
  Pallas kernels  49.8 us (97%)
  between operations  1.29 us (3%)
    pallas_call x1, Pallas kernels, per_device(): pl.pallas_call(functools.partial(kernel, scale), out_shape=(jax.ShapeDtyp...  47.7 us
    pallas_call x1, Pallas kernels, per_device(): pl.pallas_call(hand_over, out_shape=tuple((jax.ShapeDtypeStruct(v.shape,...  2.11 us

profile of v2, /device:TPU:1, one launch (start us, length us, event | category | flops | bytes accessed | tf_op | source)
XLA Modules:
  0.0 51.1 jit_solution(2767660919255298213)
XLA Ops:
  1.3 47.7 %shard_map.76 = (bf16[8,8,16,256]{3,2,1,0:T(8,128)(2,1)}, bf16[8,8,16,256]{3,2,1,0:T(8,128)(2,1)}, f32[54,128]{1,0:T(8,128)}) custom-call(s32[1,1,2]{2,1,0:T(1,128)} %lev.1, s32[1,1]{1,0:T(1,128)S(6)} %copy.8.cnt, bf16[8,8,16,256]{3,2,1,0:T(8,128)(2,1)} %bitcast.5, bf16[8,8,16,256]{3,2,1,0:T(8,128)(2,1)} %bitcast.6, bf16[27,256,256]{2,1,0:T(8,128)(2,1)} %w_hbm.1), custom_call_target="tpu_custom_call" | custom-call | tf_op jit(solution)/shard_map/pallas_call | solution.py:412
  49.0 2.1 %shard_map.77 = (bf16[8,8,16,256]{3,2,1,0:T(8,128)(2,1)}, bf16[8,8,16,256]{3,2,1,0:T(8,128)(2,1)}, f32[54,128]{1,0:T(8,128)}) custom-call(bf16[8,8,16,256]{3,2,1,0:T(8,128)(2,1)} %get-tuple-element.9.a, bf16[8,8,16,256]{3,2,1,0:T(8,128)(2,1)} %get-tuple-element.10.b, f32[54,128]{1,0:T(8,128)} %get-tuple-element.11.c), custom_call_target="tpu_custom_call" | custom-call | tf_op jit(solution)/shard_map/pallas_call | solution.py:469

commit v3 on v2

--- a/solution.py
+++ b/solution.py
@@ -129,9 +129,9 @@
         copy.start()
         started.append(copy)
 
-    for kind in range(2):
-        for i in range(8):
-            go(halo(kind, i))
+    for i in (4, 5, 6, 7, 2, 3, 0, 1):
+        go(halo(0, i))
+        go(halo(1, i))
 
     def z_of(rows):
         return lax.rem(lax.broadcasted_iota(jnp.int32, (rows, 256), 0), 16)
@@ -361,19 +361,19 @@
         if n >= 2:
             send1(*PHASES[n - 2])
     send1(*PHASES[6])
+    send1(*PHASES[7])
     loads[2].wait()
-    convolve(g_fr, ig_ref, True, 0, 1)
-    send1(*PHASES[7])
-    convolve(g_fr, ig_ref, True, 1, 4)
+    convolve(g_fr, ig_ref, True, 0, 4)
     send2x(0)
     send2x(1)
+    near_columns(2, f_halo, f_fr)
+    convolve(f_fr, out_ref, False, 0, 1)
     send2y(0)
     send2y(1)
     send2x(2)
     send2x(3)
     send3()
-    near_columns(2, f_halo, f_fr)
-    convolve(f_fr, out_ref, False, 0, 4)
+    convolve(f_fr, out_ref, False, 1, 4)
     finish()
     for c in started:
         c.wait_send()

time: 51.2 us -> 49.9 us (0.975); the launches traced: 51.1 us -> 49 us
  Pallas kernels: 49.8 us -> 47.7 us
    pallas_call x1, Pallas kernels: 47.7 us -> 45.6 us  [per_device(): pl.pallas_call(functools.partial(kernel, scale), out_shape=(jax.ShapeDtyp...]
where the time goes in v3:
time: 49.9 us; the launch traced here: 49 us
  Pallas kernels  47.7 us (96%)
  between operations  1.29 us (3%)
    pallas_call x1, Pallas kernels, per_device(): pl.pallas_call(functools.partial(kernel, scale), out_shape=(jax.ShapeDtyp...  45.6 us
    pallas_call x1, Pallas kernels, per_device(): pl.pallas_call(hand_over, out_shape=tuple((jax.ShapeDtypeStruct(v.shape,...  2.11 us

profile of v3, /device:TPU:1, one launch (start us, length us, event | category | flops | bytes accessed | tf_op | source)
XLA Modules:
  0.0 49.0 jit_solution(8574411521862593628)
XLA Ops:
  1.3 45.6 %shard_map.76 = (bf16[8,8,16,256]{3,2,1,0:T(8,128)(2,1)}, bf16[8,8,16,256]{3,2,1,0:T(8,128)(2,1)}, f32[54,128]{1,0:T(8,128)}) custom-call(s32[1,1,2]{2,1,0:T(1,128)} %lev.1, s32[1,1]{1,0:T(1,128)S(6)} %copy.8.cnt, bf16[8,8,16,256]{3,2,1,0:T(8,128)(2,1)} %bitcast.5, bf16[8,8,16,256]{3,2,1,0:T(8,128)(2,1)} %bitcast.6, bf16[27,256,256]{2,1,0:T(8,128)(2,1)} %w_hbm.1), custom_call_target="tpu_custom_call" | custom-call | tf_op jit(solution)/shard_map/pallas_call | solution.py:412
  46.9 2.1 %shard_map.77 = (bf16[8,8,16,256]{3,2,1,0:T(8,128)(2,1)}, bf16[8,8,16,256]{3,2,1,0:T(8,128)(2,1)}, f32[54,128]{1,0:T(8,128)}) custom-call(bf16[8,8,16,256]{3,2,1,0:T(8,128)(2,1)} %get-tuple-element.9.a, bf16[8,8,16,256]{3,2,1,0:T(8,128)(2,1)} %get-tuple-element.10.b, f32[54,128]{1,0:T(8,128)} %get-tuple-element.11.c), custom_call_target="tpu_custom_call" | custom-call | tf_op jit(solution)/shard_map/pallas_call | solution.py:469

commit v4 on v3

--- a/solution.py
+++ b/solution.py
@@ -48,10 +48,11 @@
 
 
 def kernel(
-    scale, lev, cnt, f_hbm, g_hbm, w_hbm, out_ref, ig_ref, wg_ref,
+    scale, lev_hbm, cnt_hbm, f_hbm, g_hbm, w_hbm, out_hbm, ig_hbm, wg_hbm,
+    lev, cnt, out_ref, ig_ref, wg_ref,
     f_own, g_own, w_all, f_fr, g_fr, f_halo, g_halo, meta, near, ft, wg,
     r0, pair, parted, qx1, qy1, ownx, owny, rx1, ry1, qx2, qy2, rx2, ry2, total, q3, r3,
-    load_sem, hs, hr, s0s, s0r, x1s, x1r, y1s, y1r, x2s, x2r, y2s, y2r, s3s, s3r,
+    load_sem, store_sem, hs, hr, s0s, s0r, x1s, x1r, y1s, y1r, x2s, x2r, y2s, y2r, s3s, s3r,
 ):
     gx, gy = lax.axis_index("gx"), lax.axis_index("gy")
     y, xl, core = lax.div(gx, 4), lax.rem(lax.div(gx, 2), 2), lax.rem(gx, 2)
@@ -79,19 +80,33 @@
         pltpu.make_async_copy(g_hbm, g_own, load_sem.at[0]),
         pltpu.make_async_copy(f_hbm, f_own, load_sem.at[1]),
         pltpu.make_async_copy(w_hbm, w_all, load_sem.at[2]),
+        pltpu.make_async_copy(lev_hbm, lev, load_sem.at[3]),
+        pltpu.make_async_copy(cnt_hbm, cnt, load_sem.at[4]),
     ]
-    for c in loads:
-        c.start()
 
     barrier = pltpu.get_barrier_semaphore()
-    for d in DIRS:
-        pl.semaphore_signal(barrier, inc=1, device_id=neighbour(d), device_id_type=MESH)
-    pl.semaphore_signal(barrier, inc=1, device_id=sibling, device_id_type=MESH)
-    for j in (1, 2, 3):
-        pl.semaphore_signal(barrier, inc=1, device_id=place(y, x_peer(j), core, z), device_id_type=MESH)
-        pl.semaphore_signal(barrier, inc=1, device_id=place(y_peer(j), x, core, z), device_id_type=MESH)
-    for j in range(1, 8):
-        pl.semaphore_signal(barrier, inc=1, device_id=place(y, x, core, z_peer(j)), device_id_type=MESH)
+    def greet(device):
+        pl.semaphore_signal(barrier, inc=1, device_id=device, device_id_type=MESH)
+
+    greet(place(y, x, core, z_peer(4)))
+    for i in (4, 5, 6, 7):
+        greet(neighbour(DIRS[i]))
+    for i in (2, 3):
+        greet(neighbour(DIRS[i]))
+    for j in (3, 5, 2, 6):
+        greet(place(y, x, core, z_peer(j)))
+    for j in (2, 1, 3):
+        greet(place(y, x_peer(j), core, z))
+        greet(place(y_peer(j), x, core, z))
+    for j in (1, 7):
+        greet(place(y, x, core, z_peer(j)))
+    for i in (0, 1):
+        greet(neighbour(DIRS[i]))
+    greet(sibling)
+    for n in (3, 4, 0, 1, 2):
+        loads[n].start()
+    loads[3].wait()
+    loads[4].wait()
 
     shift = lev[0, 0, 0].astype(F32)
     second = jnp.where(cnt[0, 0] >= 2, 1.0, 0.0).astype(F32)
@@ -152,7 +167,8 @@
     own_columns(f_own, f_fr, True)
 
     def near_columns(kind, recv, fr):
-        for i, (dx, dy) in enumerate(DIRS):
+        for i in (0, 1, 4, 5, 6, 7, 2, 3):
+            dx, dy = DIRS[i]
             if kind == 1:
                 halo(0, DIRS.index((-dx, -dy))).wait_recv()
             halo(kind, DIRS.index((-dx, -dy))).wait_recv()
@@ -334,7 +350,9 @@
 
     keep256 = jnp.where(z_of(256) < 8, 1.0, second)
 
-    def convolve(fr, dst, transposed, lo, hi):
+    stores = []
+
+    def convolve(fr, dst, out, transposed, lo, hi):
         def tile(t, _):
             acc = None
             for o in range(27):
@@ -351,6 +369,10 @@
             return 0
 
         lax.fori_loop(lo, hi, tile, 0)
+        part = pl.ds(2 * lo, 2 * (hi - lo))
+        c = pltpu.make_async_copy(dst.at[part], out.at[part], store_sem.at[len(stores)])
+        c.start()
+        stores.append(c)
 
     done = 0
     for n, (p, a) in enumerate(PHASES):
@@ -363,18 +385,21 @@
     send1(*PHASES[6])
     send1(*PHASES[7])
     loads[2].wait()
-    convolve(g_fr, ig_ref, True, 0, 4)
+    convolve(g_fr, ig_ref, ig_hbm, True, 0, 4)
     send2x(0)
     send2x(1)
     near_columns(2, f_halo, f_fr)
-    convolve(f_fr, out_ref, False, 0, 1)
+    convolve(f_fr, out_ref, out_hbm, False, 0, 1)
     send2y(0)
     send2y(1)
     send2x(2)
     send2x(3)
     send3()
-    convolve(f_fr, out_ref, False, 1, 4)
+    convolve(f_fr, out_ref, out_hbm, False, 1, 4)
     finish()
+    c = pltpu.make_async_copy(wg_ref, wg_hbm, store_sem.at[len(stores)])
+    c.start()
+    stores.append(c)
     for c in started:
         c.wait_send()
     for p, a in PHASES:
@@ -383,11 +408,13 @@
         for p in range(4):
             copy_x1(p, j).wait_send()
         copy_y2(j).wait_send()
+    for c in stores:
+        c.wait()
 
 
 def hand_over(a, b, c, a_out, b_out, c_out, a_buf, b_buf, c_buf, in_sems, out_sems):
-    moves = [(a, a_buf, a_out, pl.ds(2 * i, 2)) for i in range(4)]
-    moves += [(b, b_buf, b_out, pl.ds(2 * i, 2)) for i in range(4)]
+    moves = [(a, a_buf, a_out, pl.ds(4 * i, 4)) for i in range(2)]
+    moves += [(b, b_buf, b_out, pl.ds(4 * i, 4)) for i in range(2)]
     moves += [(c, c_buf, c_out, pl.ds(0, 2 * SHARE))]
     ins = [pltpu.make_async_copy(v.at[part], buf.at[part], in_sems.at[i]) for i, (v, buf, _, part) in enumerate(moves)]
     outs = [pltpu.make_async_copy(buf.at[part], o.at[part], out_sems.at[i]) for i, (_, buf, o, part) in enumerate(moves)]
@@ -404,8 +431,6 @@
     f = features.reshape(8, 8, 16, 256)
     g = cotangent.reshape(8, 8, 16, 256)
     scale = 1.0 / math.sqrt(1024 * lax.axis_size("gx") * lax.axis_size("gy"))
-    vmem = pl.BlockSpec(memory_space=pltpu.VMEM)
-    smem = pl.BlockSpec(memory_space=pltpu.SMEM)
     anywhere = pl.BlockSpec(memory_space=pl.ANY)
     dma = pltpu.SemaphoreType.DMA
     i16 = jnp.int16
@@ -416,9 +441,14 @@
             jax.ShapeDtypeStruct((8, 8, 16, 256), BF16),
             jax.ShapeDtypeStruct((2 * SHARE, 128), F32),
         ),
-        in_specs=[smem, smem, anywhere, anywhere, anywhere],
-        out_specs=(vmem, vmem, vmem),
+        in_specs=[anywhere] * 5,
+        out_specs=(anywhere,) * 3,
         scratch_shapes=[
+            pltpu.SMEM((1, 1, 2), jnp.int32),
+            pltpu.SMEM((1, 1), jnp.int32),
+            pltpu.VMEM((8, 8, 16, 256), BF16),
+            pltpu.VMEM((8, 8, 16, 256), BF16),
+            pltpu.VMEM((2 * SHARE, 128), F32),
             pltpu.VMEM((8, 8, 16, 256), BF16),
             pltpu.VMEM((8, 8, 16, 256), BF16),
             pltpu.VMEM((27, 256, 256), BF16),
@@ -446,7 +476,8 @@
             pltpu.VMEM((PADDED, 256), F32),
             pltpu.VMEM((8, 32, 256), i16),
             pltpu.VMEM((7, 32, 256), i16),
-            dma((3,)),
+            dma((5,)),
+            dma((4,)),
             dma((3, 8)),
             dma((3, 8)),
             dma((4, 2)),
@@ -475,8 +506,8 @@
             pltpu.VMEM(out.shape, BF16),
             pltpu.VMEM(ig.shape, BF16),
             pltpu.VMEM(wgrad.shape, F32),
-            dma((9,)),
-            dma((9,)),
+            dma((5,)),
+            dma((5,)),
         ],
     )(out, ig, wgrad)
     shape = features.shape

time: 49.9 us -> 48.6 us (0.974)
  Pallas kernels: 47.7 us -> 46.4 us
    pallas_call x1, Pallas kernels: 45.6 us -> 44.4 us  [per_device(): pl.pallas_call(functools.partial(kernel, scale), out_shape=(jax.ShapeDtyp...]
where the time goes in v4:
time: 48.6 us; the launch traced here: 47.7 us
  Pallas kernels  46.4 us (95%)
  between operations  1.29 us (3%)
    pallas_call x1, Pallas kernels, per_device(): pl.pallas_call(functools.partial(kernel, scale), out_shape=(jax.ShapeDtyp...  44.4 us
    pallas_call x1, Pallas kernels, per_device(): pl.pallas_call(hand_over, out_shape=tuple((jax.ShapeDtypeStruct(v.shape,...  2 us

profile of v4, /device:TPU:1, one launch (start us, length us, event | category | flops | bytes accessed | tf_op | source)
XLA Modules:
  0.0 47.7 jit_solution(18122601361040306567)
XLA Ops:
  1.3 44.4 %shard_map.76 = (bf16[8,8,16,256]{3,2,1,0:T(8,128)(2,1)}, bf16[8,8,16,256]{3,2,1,0:T(8,128)(2,1)}, f32[54,128]{1,0:T(8,128)}) custom-call(s32[1,1,2]{2,1,0:T(1,128)} %lev_hbm.1, s32[1,1]{1,0:T(1,128)S(6)} %copy.8.cnt_hbm, bf16[8,8,16,256]{3,2,1,0:T(8,128)(2,1)} %bitcast.5, bf16[8,8,16,256]{3,2,1,0:T(8,128)(2,1)} %bitcast.6, bf16[27,256,256]{2,1,0:T(8,128)(2,1)} %w_hbm.1), custom_call_target="tpu_custom_call" | custom-call | tf_op jit(solution)/shard_map/pallas_call | solution.py:437
  45.7 2.0 %shard_map.77 = (bf16[8,8,16,256]{3,2,1,0:T(8,128)(2,1)}, bf16[8,8,16,256]{3,2,1,0:T(8,128)(2,1)}, f32[54,128]{1,0:T(8,128)}) custom-call(bf16[8,8,16,256]{3,2,1,0:T(8,128)(2,1)} %get-tuple-element.9.a, bf16[8,8,16,256]{3,2,1,0:T(8,128)(2,1)} %get-tuple-element.10.b, f32[54,128]{1,0:T(8,128)} %get-tuple-element.11.c), custom_call_target="tpu_custom_call" | custom-call | tf_op jit(solution)/shard_map/pallas_call | solution.py:500

commit v5 on v4

--- a/solution.py
+++ b/solution.py
@@ -110,8 +110,7 @@
 
     shift = lev[0, 0, 0].astype(F32)
     second = jnp.where(cnt[0, 0] >= 2, 1.0, 0.0).astype(F32)
-    eight = lax.broadcasted_iota(jnp.int32, (8, 256), 0)
-    meta[...] = jnp.where(eight < 4, shift, second)
+    meta[...] = jnp.where(lax.broadcasted_iota(jnp.int32, (2, 128), 0) == 0, shift, second)
     loads[0].wait()
     loads[1].wait()
     pl.semaphore_wait(barrier, 22)
@@ -177,14 +176,15 @@
                 jnp.logical_and(gx + dx >= 0, gx + dx < 16), jnp.logical_and(gy + dy >= 0, gy + dy < 16)
             )
             valid = jnp.where(inside, 1.0, 0.0).astype(F32)
-            higher_by = near[i, 0:1, :] - shift
+            facts = jnp.concatenate([near[i], near[i]], axis=1)
+            higher_by = facts[0:1] - shift
             level = jnp.where(higher_by == 0.0, valid, 0.0)
             above = jnp.where(higher_by == 1.0, valid, 0.0)
             below = jnp.where(higher_by == -1.0, valid, 0.0)
             rows = n * 16
             zr = z_of(rows)
             v = recv[COLS[i] : COLS[i] + n].reshape(rows, 256).astype(F32)
-            v = v * jnp.where(zr < 8, 1.0, near[i, 4:5, :])
+            v = v * jnp.where(zr < 8, 1.0, facts[1:2])
             swapped = pltpu.roll(v, 8, 0) if n == 1 else None
             up8 = swapped if n == 1 else pltpu.roll(v, 8, 0)
             down8 = swapped if n == 1 else pltpu.roll(v, rows - 8, 0)
@@ -456,8 +456,8 @@
             pltpu.VMEM((3, 10, 10, 16, 256), BF16),
             pltpu.VMEM((36, 16, 256), BF16),
             pltpu.VMEM((36, 16, 256), BF16),
-            pltpu.VMEM((8, 256), F32),
-            pltpu.VMEM((8, 8, 256), F32),
+            pltpu.VMEM((2, 128), F32),
+            pltpu.VMEM((8, 2, 128), F32),
             pltpu.VMEM((256, 1024), BF16),
             pltpu.VMEM((6912, 256), F32),
             pltpu.VMEM((4, 2, 2 * HALF, 256), F32),

time: 48.6 us -> 47.6 us (0.979)
  Pallas kernels: 46.4 us -> 45.4 us
    pallas_call x1, Pallas kernels: 44.4 us -> 43.4 us  [per_device(): pl.pallas_call(functools.partial(kernel, scale), out_shape=(jax.ShapeDtyp...]
where the time goes in v5:
time: 47.6 us; the launch traced here: 46.7 us
  Pallas kernels  45.4 us (95%)
  between operations  1.29 us (3%)
    pallas_call x1, Pallas kernels, per_device(): pl.pallas_call(functools.partial(kernel, scale), out_shape=(jax.ShapeDtyp...  43.4 us
    pallas_call x1, Pallas kernels, per_device(): pl.pallas_call(hand_over, out_shape=tuple((jax.ShapeDtypeStruct(v.shape,...  2 us

profile of v5, /device:TPU:1, one launch (start us, length us, event | category | flops | bytes accessed | tf_op | source)
XLA Modules:
  0.0 46.7 jit_solution(2248619138687693710)
XLA Ops:
  1.3 43.4 %shard_map.76 = (bf16[8,8,16,256]{3,2,1,0:T(8,128)(2,1)}, bf16[8,8,16,256]{3,2,1,0:T(8,128)(2,1)}, f32[54,128]{1,0:T(8,128)}) custom-call(s32[1,1,2]{2,1,0:T(1,128)} %lev_hbm.1, s32[1,1]{1,0:T(1,128)S(6)} %copy.8.cnt_hbm, bf16[8,8,16,256]{3,2,1,0:T(8,128)(2,1)} %bitcast.5, bf16[8,8,16,256]{3,2,1,0:T(8,128)(2,1)} %bitcast.6, bf16[27,256,256]{2,1,0:T(8,128)(2,1)} %w_hbm.1), custom_call_target="tpu_custom_call" | custom-call | tf_op jit(solution)/shard_map/pallas_call | solution.py:437
  44.7 2.0 %shard_map.77 = (bf16[8,8,16,256]{3,2,1,0:T(8,128)(2,1)}, bf16[8,8,16,256]{3,2,1,0:T(8,128)(2,1)}, f32[54,128]{1,0:T(8,128)}) custom-call(bf16[8,8,16,256]{3,2,1,0:T(8,128)(2,1)} %get-tuple-element.9.a, bf16[8,8,16,256]{3,2,1,0:T(8,128)(2,1)} %get-tuple-element.10.b, f32[54,128]{1,0:T(8,128)} %get-tuple-element.11.c), custom_call_target="tpu_custom_call" | custom-call | tf_op jit(solution)/shard_map/pallas_call | solution.py:500
